TPU v7x, 32 devices: a whole 2x2x4 slice. The times are simulated.
32 devices in a mesh: lon: 16 (over z, y, x), lat: 2 (over core).
Axes of the slice: x: 2, y: 2, z: 4, core: 2. Of those that a mesh axis runs over, the one named last changes fastest.
Arguments:
- field: bfloat16 [128, 256, 256], P('lat', 'lon'), may hold values from -6 to 6
- cotangent: bfloat16 [128, 256, 256], P('lat', 'lon'), may hold values from -6 to 6
- lon_kernel: float32 [31, 256], replicated, may hold values from -1 to 1
- lat_kernel: float32 [31, 256], replicated, may hold values from -1 to 1
- w_in: bfloat16 [256, 1024], replicated, may hold values from -0.375 to 0.375
- w_out: bfloat16 [1024, 256], replicated, may hold values from -0.1875 to 0.1875
Outputs:
- result: bfloat16 [128, 256, 256], P('lat', 'lon')
- d_field: bfloat16 [128, 256, 256], P('lat', 'lon')
- grad_in: float32 [256, 1024], replicated
- grad_out: float32 [1024, 256], replicated
- grad_lat: float32 [31, 256], replicated
- grad_lon: float32 [31, 256], replicated
All inputs are finite; a program needn't handle non-finite values.
Results may differ from a plain program's by a relative error of at most 0.007.
Values may be sent and summed in bfloat16 or wider, within the bound.
A program may use at most 64 MiB of HBM per device.

v0:
```python
import math

import jax
import jax.numpy as jnp
from jax import lax
from jax.sharding import PartitionSpec as P

KW = 31
HALF = 15


def with_halo(value, sides, width, wrap):
    for axis, dim in sides:
        size, length = (lax.axis_size(axis), value.shape[dim])
        up = [(i, (i + 1) % size) for i in range(size if wrap else size - 1)]
        down = [(j, i) for i, j in up]
        last = lax.slice_in_dim(value, length - width, length, axis=dim)
        initial = lax.slice_in_dim(value, 0, width, axis=dim)
        before = lax.ppermute(last, axis, up)
        after = lax.ppermute(initial, axis, down)
        value = jnp.concatenate([before, value, after], axis=dim)
    return value


def kernel_taps(padded, kernel, along, length):
    total = None
    for offset in range(kernel.shape[0]):
        piece = (
            lax.slice_in_dim(padded, offset, offset + length, axis=along).astype(jnp.float32)
            * kernel[offset]
        )
        total = piece if total is None else total + piece
    return total


def kernel_grad(padded, grad, along, length):
    grad_wide = grad.astype(jnp.float32)
    rows_out = []
    for offset in range(KW):
        piece = lax.slice_in_dim(padded, offset, offset + length, axis=along).astype(jnp.float32)
        rows_out.append(jnp.sum(piece * grad_wide, axis=(0, 1)))
    return jnp.stack(rows_out)


def mlp_block(mixed_rows, field_rows, cot_rows, w_in, w_out, scale):
    rms = jnp.sqrt(jnp.mean(mixed_rows * mixed_rows, axis=-1, keepdims=True) + 1e-06)
    unit = mixed_rows / rms
    normed = unit.astype(jnp.bfloat16)
    pre = jnp.dot(normed, w_in, preferred_element_type=jnp.float32)
    act_wide, gelu_back = jax.vjp(jax.nn.gelu, pre)
    act = act_wide.astype(jnp.bfloat16)
    result = (
        field_rows.astype(jnp.float32) + jnp.dot(act, w_out, preferred_element_type=jnp.float32)
    ).astype(jnp.bfloat16)
    d_act = lax.dot_general(
        cot_rows, w_out, (((1,), (1,)), ((), ())), preferred_element_type=jnp.float32
    )
    d_pre = gelu_back(d_act)[0].astype(jnp.bfloat16)
    grad_out = scale * lax.dot_general(
        act, cot_rows, (((0,), (0,)), ((), ())), preferred_element_type=jnp.float32
    )
    return (result, normed, unit, rms, d_pre, grad_out)


def on_device(field, cotangent, lon_kernel, lat_kernel, w_in, w_out):
    lat_dev, lon_dev, chans = field.shape
    n_lon = lax.axis_size("lon")
    scale = 1.0 / math.sqrt(lat_dev * lon_dev * n_lon * lax.axis_size("lat"))
    field_cycle = with_halo(field, (("lon", 1),), HALF, True)
    along = kernel_taps(field_cycle, lon_kernel, 1, lon_dev).astype(jnp.bfloat16)
    along_band = with_halo(along, (("lat", 0),), HALF, False)
    mixed = kernel_taps(along_band, lat_kernel, 0, lat_dev)
    cells = lat_dev * lon_dev
    cot_rows = cotangent.reshape(cells, chans)
    result, normed, unit, rms, d_pre, grad_out = mlp_block(
        mixed.reshape(cells, chans), field.reshape(cells, chans), cot_rows, w_in, w_out, scale
    )
    grad_in = scale * lax.dot_general(
        normed, d_pre, (((0,), (0,)), ((), ())), preferred_element_type=jnp.float32
    )
    d_norm = lax.dot_general(
        d_pre, w_in, (((1,), (1,)), ((), ())), preferred_element_type=jnp.float32
    )
    d_mixed = ((d_norm - unit * jnp.mean(d_norm * unit, axis=-1, keepdims=True)) / rms).astype(
        jnp.bfloat16
    )
    d_mixed = d_mixed.reshape(lat_dev, lon_dev, chans)
    grad_lat = scale * kernel_grad(along_band, d_mixed, 0, lat_dev)
    d_band = with_halo(d_mixed, (("lat", 0),), HALF, False)
    d_along = kernel_taps(d_band, lat_kernel[::-1], 0, lat_dev).astype(jnp.bfloat16)
    d_cycle = with_halo(d_along, (("lon", 1),), HALF, True)
    conv_back = kernel_taps(d_cycle, lon_kernel[::-1], 1, lon_dev)
    grad_lon = scale * kernel_grad(field_cycle, d_along, 1, lon_dev)
    d_field = (cotangent.astype(jnp.float32) + conv_back).astype(jnp.bfloat16)
    grad_in, grad_out, grad_lat, grad_lon = lax.psum(
        (grad_in, grad_out, grad_lat, grad_lon), ("lon", "lat")
    )
    return (result.reshape(lat_dev, lon_dev, chans), d_field, grad_in, grad_out, grad_lat, grad_lon)


def solution(mesh):
    placed = (P("lat", "lon", None), P("lat", "lon", None), P(), P(), P(), P())
    return jax.shard_map(
        on_device,
        mesh=mesh,
        in_specs=placed,
        out_specs=(P("lat", "lon", None), P("lat", "lon", None), P(), P(), P(), P()),
        check_vma=False,
    )
```

profile of v0, /device:TPU:0, one launch (start us, length us, event | category | flops | bytes accessed | tf_op | source)
XLA Modules:
  0.0 251.3 jit_solution(5320542791609633994)
XLA Ops:
  8.7 3.0 %collective-permute-start = (bf16[64,15,256]{2,1,0:T(8,128)(2,1)S(1)}, bf16[64,15,256]{2,1,0:T(8,128)(2,1)S(1)}, u32[]{:S(2)}, u32[]{:S(2)}) collective-permute-start(bf16[64,15,256]{2,1,0:T(8,128)(2,1)S(1)} %get-tuple-element.82), channel_id=1, source_target_pairs={{0,2},{2,4},{4,6},{6,8},{8,10},{10,12},{12,14},{14,16},{16,18},{18... | collective-permute-start | bytes 1474568 | tf_op jit(solution)/shard_map/ppermute | solution.py:19
  11.7 4.1 %collective-permute-start.1 = (bf16[64,15,256]{2,1,0:T(8,128)(2,1)S(1)}, bf16[64,15,256]{2,1,0:T(8,128)(2,1)S(1)}, u32[]{:S(2)}, u32[]{:S(2)}) collective-permute-start(bf16[64,15,256]{2,1,0:T(8,128)(2,1)S(1)} %get-tuple-element.83), channel_id=1, source_target_pairs={{2,0},{4,2},{6,4},{8,6},{10,8},{12,10},{14,12},{16,14},{18,16},{20... | collective-permute-start | bytes 1474568 | tf_op jit(solution)/shard_map/ppermute | solution.py:20
  19.1 1.6 fusion.273
  20.8 15.2 %collective-permute-done.1 = bf16[64,15,256]{2,1,0:T(8,128)(2,1)S(1)} collective-permute-done((bf16[64,15,256]{2,1,0:T(8,128)(2,1)S(1)}, bf16[64,15,256]{2,1,0:T(8,128)(2,1)S(1)}, u32[]{:S(2)}, u32[]{:S(2)}) %collective-permute-start.1) | collective-permute-done | bytes 491552 | tf_op jit(solution)/shard_map/ppermute | solution.py:20
  36.4 5.4 %fusion.38 = bf16[64,16,256]{2,1,0:T(8,128)(2,1)S(1)} fusion(bf16[64,16,256]{2,1,0:T(8,128)(2,1)S(1)} %copy-done.1, f32[256]{0:T(256)S(1)} %bitcast.237, f32[256]{0:T(256)S(1)} %bitcast.239, f32[256]{0:T(256)S(1)} %bitcast.181, f32[256]{0:T(256)S(1)} %bitcast.183, f32[256]{0:T(256)S(1)} %bitcast.185, f32[256]{0:T(256)S(1)} %bitcast.187, ...), kind=kLoop, calls=%fused_computation.309 | loop fusion | flops 36175872 | bytes 9436160 | tf_op jit(solution)/shard_map/convert_element_type | solution.py:70
  46.5 21.4 %multiply_reduce_fusion.1 = (f32[64,16]{1,0:T(8,128)S(1)}, f32[64,16,256]{2,1,0:T(8,128)}) fusion(f32[256]{0:T(256)S(1)} %bitcast.295, bf16[15,16,256]{2,1,0:T(8,128)(2,1)S(1)} %collective-permute-done.3, bf16[64,16,256]{2,1,0:T(8,128)(2,1)S(1)} %fusion.38, f32[256]{0:T(256)S(1)} %bitcast.297, f32[256]{0:T(256)S(1)} %bitcast.243, f32[256]{0:T(256)S(1)} %bitcast.245, ...), kind=kLoop, calls=%fused_computation.438 | loop fusion | flops 32504832 | bytes 1854464 | tf_op jit(solution)/shard_map/reduce_sum | solution.py:46
  70.3 2.5 %convolution_multiply_fusion = f32[1024,256]{1,0:T(8,128)} fusion(bf16[1024,256]{1,0:T(8,128)(2,1)S(1)} %bitcast.176, f32[1024,1024]{1,0:T(8,128)S(1)} %fusion.265), kind=kOutput, calls=%fused_computation.214 | convolution fusion | flops 546570240 | bytes 5767168 | tf_op jit(solution)/shard_map/dot_general | solution.py:59
  72.8 3.4 %fusion.6 = bf16[1024,1024]{1,0:T(8,128)(2,1)S(1)} fusion(f32[1024,1024]{1,0:T(8,128)S(1)} %fusion.265, bf16[1024,256]{1,0:T(8,128)(2,1)S(1)} %bitcast.177, bf16[1024,256]{1,0:T(8,128)(2,1)S(1)} %copy-done.82), kind=kOutput, calls=%fused_computation.72 | convolution fusion | flops 557842432 | bytes 7340032 | tf_op jit(solution)/shard_map/dot_general | solution.py:55
  77.6 1.7 convolution_multiply_fusion.1
  79.3 2.8 %multiply_reduce_fusion = (f32[1024]{0:T(1024)S(1)}, f32[1024,256]{1,0:T(8,128)S(1)}) fusion(f32[1024,256]{1,0:T(8,128)} %copy-done.2, bf16[1024,1024]{1,0:T(8,128)(2,1)} %copy-done.4, bf16[256,1024]{1,0:T(8,128)(2,1)S(1)} %copy-done), kind=kOutput, calls=%fused_computation.437 | convolution fusion | flops 537394176 | bytes 4722688 | tf_op jit(solution)/shard_map/dot_general | solution.py:81
  82.4 2.3 fusion.7
  84.8 9.1 %fusion.115 = (f32[256]{0:T(256)}, f32[256]{0:T(256)}, f32[256]{0:T(256)}, f32[256]{0:T(256)}, f32[256]{0:T(256)}, /*index=5*/f32[256]{0:T(256)}, f32[256]{0:T(2...) fusion(bf16[15,16,256]{2,1,0:T(8,128)(2,1)S(1)} %collective-permute-done.3, ...), kind=kLoop, calls=%fused_computation.386 | loop fusion | flops 11007744 | bytes 3286016 | tf_op jit(solution)/shard_map/reduce_sum | solution.py:41
  95.8 4.3 %collective-permute-start.4 = (bf16[15,16,256]{2,1,0:T(8,128)(2,1)S(1)}, bf16[15,16,256]{2,1,0:T(8,128)(2,1)}, u32[]{:S(2)}, u32[]{:S(2)}) collective-permute-start(bf16[15,16,256]{2,1,0:T(8,128)(2,1)S(1)} %bitcast.178), channel_id=1, source_target_pairs={{0,1},{2,3},{4,5},{6,7},{8,9},{10,11},{12,13},{14,15},{16,17},{18,... | collective-permute-start | bytes 368648 | tf_op jit(solution)/shard_map/ppermute | solution.py:19
  103.3 2.2 stack.223
  105.5 19.1 %fusion.163 = (f32[256]{0:T(256)S(1)}, f32[256]{0:T(256)S(1)}, f32[256]{0:T(256)S(1)}, f32[256]{0:T(256)S(1)}, f32[256]{0:T(256)S(1)}, /*index=5*/f32[256]{0:T(2...) fusion(bf16[64,31,256]{2,1,0:T(8,128)(2,1)S(1)} %constant_dynam, ...), kind=kLoop, calls=%fused_computation.434 | loop fusion | flops 44298496 | bytes 9205760 | tf_op jit(solution)/shard_map/reduce_sum | solution.py:41
  126.1 1.5 collective-permute-start.6
  127.6 4.1 %collective-permute-start.7 = (bf16[64,15,256]{2,1,0:T(8,128)(2,1)}, bf16[64,15,256]{2,1,0:T(8,128)(2,1)S(1)}, u32[]{:S(2)}, u32[]{:S(2)}) collective-permute-start(bf16[64,15,256]{2,1,0:T(8,128)(2,1)} %get-tuple-element.77), channel_id=1, source_target_pairs={{2,0},{4,2},{6,4},{8,6},{10,8},{12,10},{14,12},{16,14},{18,16},{20... | collective-permute-start | bytes 1474568 | tf_op jit(solution)/shard_map/ppermute | solution.py:20
  131.7 1.9 fusion.147
  133.6 1.5 fusion.146
  135.2 52.1 %all-reduce = (f32[31,256]{1,0:T(8,128)}, f32[31,256]{1,0:T(8,128)}) all-reduce(f32[31,256]{1,0:T(8,128)S(1)} %get-tuple-element.149, f32[31,256]{1,0:T(8,128)S(1)} %get-tuple-element.148), channel_id=1, replica_groups=mesh['lon'=16,'lat'=2] {'lon','lat'}, use_global_device_ids=true, to_apply=%region_35.0 | all-reduce | flops 15872 | bytes 126976 | tf_op jit(solution)/shard_map/psum | solution.py:95
  187.6 7.0 %fusion.165 = bf16[64,16,256]{2,1,0:T(8,128)(2,1)} fusion(bf16[64,16,256]{2,1,0:T(8,128)(2,1)S(1)} %get-tuple-element.72, bf16[64,16,256]{2,1,0:T(8,128)(2,1)S(1)} %copy-done.10, bf16[64,15,256]{2,1,0:T(8,128)(2,1)S(1)} %collective-permute-done.7, bf16[64,15,256]{2,1,0:T(8,128)(2,1)S(1)} %collective-permute-done.6, f32[256]{0:T(256)S(1)} %bitcast.238, ...), kind=kLoop, calls=%fused_computation.440 | loop fusion | flops 48496640 | bytes 2587648 | tf_op jit(solution)/shard_map/convert_element_type | solution.py:94
  194.5 45.3 %all-reduce.4.cloned.1.call-done = (f32[256,1024]{1,0:T(8,128)}, f32[1024,256]{1,0:T(8,128)}) async-done(((f32[256,1024]{1,0:T(8,128)}, f32[1024,256]{1,0:T(8,128)}), (f32[256,1024]{1,0:T(8,128)}, f32[1024,256]{1,0:T(8,128)})) %all-reduce.4.cloned.1.call-update) | async-done | bytes 2097168 | tf_op jit(solution)/shard_map/psum | solution.py:95
  239.9 2.3 copy.15
  242.2 2.3 copy.16
  (199 shorter events, 19.8 us)
Async XLA Ops:
  7.2 232.7 %all-reduce.4.cloned.1.call-start = ((), (), s32[]{:S(2)}) async-start(), calls=%async_computation | async-start | bytes 4194304 | tf_op jit(solution)/shard_map/psum | solution.py:95
  8.7 27.4 %collective-permute-start = (bf16[64,15,256]{2,1,0:T(8,128)(2,1)S(1)}, bf16[64,15,256]{2,1,0:T(8,128)(2,1)S(1)}, u32[]{:S(2)}, u32[]{:S(2)}) collective-permute-start(bf16[64,15,256]{2,1,0:T(8,128)(2,1)S(1)} %get-tuple-element.82), channel_id=1, source_target_pairs={{0,2},{2,4},{4,6},{6,8},{8,10},{10,12},{12,14},{14,16},{16,18},{18... | collective-permute-start | bytes 1474568 | tf_op jit(solution)/shard_map/ppermute | solution.py:19
  11.7 24.4 %collective-permute-start.1 = (bf16[64,15,256]{2,1,0:T(8,128)(2,1)S(1)}, bf16[64,15,256]{2,1,0:T(8,128)(2,1)S(1)}, u32[]{:S(2)}, u32[]{:S(2)}) collective-permute-start(bf16[64,15,256]{2,1,0:T(8,128)(2,1)S(1)} %get-tuple-element.83), channel_id=1, source_target_pairs={{2,0},{4,2},{6,4},{8,6},{10,8},{12,10},{14,12},{16,14},{18,16},{20... | collective-permute-start | bytes 1474568 | tf_op jit(solution)/shard_map/ppermute | solution.py:20
  41.8 3.9 %collective-permute-start.2 = (bf16[15,16,256]{2,1,0:T(8,128)(2,1)S(1)}, bf16[15,16,256]{2,1,0:T(8,128)(2,1)S(1)}, u32[]{:S(2)}, u32[]{:S(2)}) collective-permute-start(bf16[15,16,256]{2,1,0:T(8,128)(2,1)S(1)} %get-tuple-element.80), channel_id=1, source_target_pairs={{0,1},{2,3},{4,5},{6,7},{8,9},{10,11},{12,13},{14,15},{16,17},{18,... | collective-permute-start | bytes 368648 | tf_op jit(solution)/shard_map/ppermute | solution.py:19
  43.1 3.2 %collective-permute-start.3 = (bf16[15,16,256]{2,1,0:T(8,128)(2,1)S(1)}, bf16[15,16,256]{2,1,0:T(8,128)(2,1)S(1)}, u32[]{:S(2)}, u32[]{:S(2)}) collective-permute-start(bf16[15,16,256]{2,1,0:T(8,128)(2,1)S(1)} %get-tuple-element.81), channel_id=1, source_target_pairs={{1,0},{3,2},{5,4},{7,6},{9,8},{11,10},{13,12},{15,14},{17,16},{19,... | collective-permute-start | bytes 368648 | tf_op jit(solution)/shard_map/ppermute | solution.py:20
  94.5 10.9 %collective-permute-start.5 = (bf16[15,16,256]{2,1,0:T(8,128)(2,1)}, bf16[15,16,256]{2,1,0:T(8,128)(2,1)}, u32[]{:S(2)}, u32[]{:S(2)}) collective-permute-start(bf16[15,16,256]{2,1,0:T(8,128)(2,1)} %bitcast.68), channel_id=1, source_target_pairs={{1,0},{3,2},{5,4},{7,6},{9,8},{11,10},{13,12},{15,14},{17,16},{19,... | collective-permute-start | bytes 368648 | tf_op jit(solution)/shard_map/ppermute | solution.py:20
  95.8 9.7 %collective-permute-start.4 = (bf16[15,16,256]{2,1,0:T(8,128)(2,1)S(1)}, bf16[15,16,256]{2,1,0:T(8,128)(2,1)}, u32[]{:S(2)}, u32[]{:S(2)}) collective-permute-start(bf16[15,16,256]{2,1,0:T(8,128)(2,1)S(1)} %bitcast.178), channel_id=1, source_target_pairs={{0,1},{2,3},{4,5},{6,7},{8,9},{10,11},{12,13},{14,15},{16,17},{18,... | collective-permute-start | bytes 368648 | tf_op jit(solution)/shard_map/ppermute | solution.py:19
  124.6 62.7 %copy-start.10 = (bf16[64,16,256]{2,1,0:T(8,128)(2,1)S(1)}, bf16[64,16,256]{2,1,0:T(8,128)(2,1)}, u32[]{:S(2)}) copy-start(bf16[64,16,256]{2,1,0:T(8,128)(2,1)} %param.7) | copy-start | bytes 1572868
  124.6 62.7 %copy-start.12 = (f32[1,256]{1,0:T(1,128)S(1)}, f32[1,256]{1,0:T(1,128)}, u32[]{:S(2)}) copy-start(f32[1,256]{1,0:T(1,128)} %copy-done.11) | copy-start | bytes 3076
  124.7 62.7 %copy-start.14 = (f32[1,256]{1,0:T(1,128)S(1)}, f32[1,256]{1,0:T(1,128)}, u32[]{:S(2)}) copy-start(f32[1,256]{1,0:T(1,128)} %copy-done.13) | copy-start | bytes 3076
  124.7 62.7 %copy-start.16 = (f32[1,256]{1,0:T(1,128)S(1)}, f32[1,256]{1,0:T(1,128)}, u32[]{:S(2)}) copy-start(f32[1,256]{1,0:T(1,128)} %copy-done.15) | copy-start | bytes 3076
  124.7 62.7 %copy-start.18 = (f32[1,256]{1,0:T(1,128)S(1)}, f32[1,256]{1,0:T(1,128)}, u32[]{:S(2)}) copy-start(f32[1,256]{1,0:T(1,128)} %copy-done.17) | copy-start | bytes 3076
  124.7 62.7 %copy-start.20 = (f32[1,256]{1,0:T(1,128)S(1)}, f32[1,256]{1,0:T(1,128)}, u32[]{:S(2)}) copy-start(f32[1,256]{1,0:T(1,128)} %copy-done.19) | copy-start | bytes 3076
  124.7 62.7 %copy-start.22 = (f32[1,256]{1,0:T(1,128)S(1)}, f32[1,256]{1,0:T(1,128)}, u32[]{:S(2)}) copy-start(f32[1,256]{1,0:T(1,128)} %copy-done.21) | copy-start | bytes 3076
  124.7 62.7 %copy-start.24 = (f32[1,256]{1,0:T(1,128)S(1)}, f32[1,256]{1,0:T(1,128)}, u32[]{:S(2)}) copy-start(f32[1,256]{1,0:T(1,128)} %copy-done.23) | copy-start | bytes 3076
  124.7 62.7 %copy-start.26 = (f32[1,256]{1,0:T(1,128)S(1)}, f32[1,256]{1,0:T(1,128)}, u32[]{:S(2)}) copy-start(f32[1,256]{1,0:T(1,128)} %copy-done.25) | copy-start | bytes 3076
  124.7 62.7 %copy-start.28 = (f32[1,256]{1,0:T(1,128)S(1)}, f32[1,256]{1,0:T(1,128)}, u32[]{:S(2)}) copy-start(f32[1,256]{1,0:T(1,128)} %copy-done.27) | copy-start | bytes 3076
  124.7 62.7 %copy-start.30 = (f32[1,256]{1,0:T(1,128)S(1)}, f32[1,256]{1,0:T(1,128)}, u32[]{:S(2)}) copy-start(f32[1,256]{1,0:T(1,128)} %copy-done.29) | copy-start | bytes 3076
  124.7 62.7 %copy-start.32 = (f32[1,256]{1,0:T(1,128)S(1)}, f32[1,256]{1,0:T(1,128)}, u32[]{:S(2)}) copy-start(f32[1,256]{1,0:T(1,128)} %copy-done.31) | copy-start | bytes 3076
  124.8 62.7 %copy-start.34 = (f32[1,256]{1,0:T(1,128)S(1)}, f32[1,256]{1,0:T(1,128)}, u32[]{:S(2)}) copy-start(f32[1,256]{1,0:T(1,128)} %copy-done.33) | copy-start | bytes 3076
  124.8 62.7 %copy-start.36 = (f32[1,256]{1,0:T(1,128)S(1)}, f32[1,256]{1,0:T(1,128)}, u32[]{:S(2)}) copy-start(f32[1,256]{1,0:T(1,128)} %copy-done.35) | copy-start | bytes 3076
  124.8 62.7 %copy-start.38 = (f32[1,256]{1,0:T(1,128)S(1)}, f32[1,256]{1,0:T(1,128)}, u32[]{:S(2)}) copy-start(f32[1,256]{1,0:T(1,128)} %copy-done.37) | copy-start | bytes 3076
  126.1 61.3 %collective-permute-start.6 = (bf16[64,15,256]{2,1,0:T(8,128)(2,1)}, bf16[64,15,256]{2,1,0:T(8,128)(2,1)S(1)}, u32[]{:S(2)}, u32[]{:S(2)}) collective-permute-start(bf16[64,15,256]{2,1,0:T(8,128)(2,1)} %get-tuple-element.76), channel_id=1, source_target_pairs={{0,2},{2,4},{4,6},{6,8},{8,10},{10,12},{12,14},{14,16},{16,18},{18... | collective-permute-start | bytes 1474568 | tf_op jit(solution)/shard_map/ppermute | solution.py:19
  127.6 59.8 %collective-permute-start.7 = (bf16[64,15,256]{2,1,0:T(8,128)(2,1)}, bf16[64,15,256]{2,1,0:T(8,128)(2,1)S(1)}, u32[]{:S(2)}, u32[]{:S(2)}) collective-permute-start(bf16[64,15,256]{2,1,0:T(8,128)(2,1)} %get-tuple-element.77), channel_id=1, source_target_pairs={{2,0},{4,2},{6,4},{8,6},{10,8},{12,10},{14,12},{16,14},{18,16},{20... | collective-permute-start | bytes 1474568 | tf_op jit(solution)/shard_map/ppermute | solution.py:20
  (69 other events, 1735.6 us)
Sparse Core Ops, SparseCore 0:
  100.3 139.5 all-reduce.3
where the time goes:
time: 252 us; the launch traced here: 251 us
  other arithmetic  70 us (28%)
  waiting for transfers between devices  61.3 us (24%)
  blocking collectives  52.1 us (21%)
  starting transfers between devices  21.1 us (8%)
  local copies, waits for them, and re-layouts  18 us (7%)
  between operations  15.4 us (6%)
  matrix products  13.5 us (5%)
    psum x1, blocking collectives, on_device(): lax.psum((grad_in, grad_out, grad_lat, grad_lon), ('lon', 'lat'))  52.1 us
    psum x1, waiting for transfers between devices, on_device(): lax.psum((grad_in, grad_out, grad_lat, grad_lon), ('lon', 'lat'))  45.3 us
    reduce_sum x7, other arithmetic, kernel_grad(): rows_out.append(jnp.sum(piece * grad_wide, axis=(0, 1)))  34.7 us
    reduce_sum x1, other arithmetic, mlp_block(): jnp.mean(mixed_rows * mixed_rows, axis=-1, keepdims=True) + 1e-06  21.4 us
    ppermute x4, waiting for transfers between devices, with_halo(): after = lax.ppermute(initial, axis, down)  15.9 us
    ppermute x4, starting transfers between devices, with_halo(): after = lax.ppermute(initial, axis, down)  10.9 us
    ppermute x4, starting transfers between devices, with_halo(): before = lax.ppermute(last, axis, up)  10.1 us
    unnamed x171, local copies, waits for them, and re-layouts  7.65 us
  transfers between devices with their start and end apart: 9, of which 3 were waited for; matrix products, arithmetic and copies ran while one was open for 17% of the time, Pallas kernels for 0%

commit v1 on v0

v1 whole, which is shorter than its diff:
```python
import functools
import math

import jax
import jax.numpy as jnp
from jax import lax
from jax.experimental import pallas as pl
from jax.experimental.pallas import tpu as pltpu
from jax.sharding import PartitionSpec as P

KW = 31
HALF = 15
BF = jnp.bfloat16
F32 = jnp.float32
CH = 4
ROOT = math.sqrt(2.0 / math.pi)


def kernel(
    n_lon, n_lat, subs,
    field, cot, lon_k, lat_k, w_in, w_out,
    result, d_field, out_big, out_small,
    xpad, ypad, aband, dband, mixed, abf, dalbf, frecv, drecv, arecv, mrecv,
    wlon, wlat, w_in_t, w_out_t, act, dpre, normed, dmbf,
    part_b, lrecv_b, pair_b, nrecv_b, all_b,
    part_s, lrecv_s, pair_s, nrecv_s, all_s,
    f_ss, f_rs, d_ss, d_rs, a_ss, a_rs, m_ss, m_rs,
    b_lss, b_lrs, b_nss, b_nrs, b_ass, b_ars, b_gss, b_grs,
    s_lss, s_lrs, s_nss, s_nrs, s_ass, s_ars, s_gss, s_grs,
):
    lat_dev, lon_dev, chans = field.shape
    halves = chans // 128
    hidden = w_in.shape[1]
    rows = lat_dev // CH
    me = lax.axis_index("lon")
    my = lax.axis_index("lat")
    right = lax.rem(me + 1, n_lon)
    left = lax.rem(me + n_lon - 1, n_lon)

    def remote(src, dst, ss, rs, lon, lat):
        return pltpu.make_async_remote_copy(
            src_ref=src, dst_ref=dst, send_sem=ss, recv_sem=rs,
            device_id=(lon, lat), device_id_type=pl.DeviceIdType.MESH,
        )

    barrier = pltpu.get_barrier_semaphore()

    @pl.loop(1, n_lon)
    def _(p):
        pl.semaphore_signal(barrier, inc=1, device_id=(lax.rem(me + p, n_lon), my),
                            device_id_type=pl.DeviceIdType.MESH)

    @pl.loop(1, n_lat)
    def _(p):
        pl.semaphore_signal(barrier, inc=1, device_id=(me, lax.rem(my + p, n_lat)),
                            device_id_type=pl.DeviceIdType.MESH)

    pl.semaphore_wait(barrier, n_lon + n_lat - 2)

    def lon_halo(src, dst, ss, rs, q):
        part = pl.ds(q * rows, rows)
        return (
            remote(src.at[part], dst.at[0, part], ss.at[0, q], rs.at[0, q], right, my),
            remote(src.at[part], dst.at[1, part], ss.at[1, q], rs.at[1, q], left, my),
        )

    def widen(src, pad, row0, count, col):
        @pl.loop(0, count)
        def _(i):
            v = src[row0 + i].astype(F32)
            for h in range(halves):
                pad[h, row0 + i, col:col + lon_dev, :] = v[:, h * 128:(h + 1) * 128]

    field_halo = [lon_halo(field, frecv, f_ss, f_rs, q) for q in range(CH)]
    for pair in field_halo:
        for c in pair:
            c.start()

    for h in range(halves):
        for k in range(KW):
            lanes = slice(h * 128, (h + 1) * 128)
            wlon[h, k] = jnp.broadcast_to(lon_k[k:k + 1, lanes], (8, 128))
            wlat[h, k] = jnp.broadcast_to(lat_k[k:k + 1, lanes], (8, 128))
    for b in range(hidden // 256):
        blk = slice(b * 256, (b + 1) * 256)
        w_in_t[blk, :] = w_in[:, blk].T
        w_out_t[:, blk] = w_out[blk, :].T
    widen(field, xpad, 0, lat_dev, lon_dev)

    def lon_taps(pad, wide, i, h, flip):
        lo = jnp.zeros((8, 128), F32)
        hi = jnp.zeros((8, 128), F32)
        for k in range(KW):
            off = 31 - k if flip else k + 1
            lo = lo + pad[h, i, off:off + 8, :] * wide[k]
            hi = hi + pad[h, i, off + 8:off + 16, :] * wide[k]
        return jnp.concatenate([lo, hi], axis=0)

    band = [[0, HALF], [HALF + lat_dev, HALF]]
    for q in range(CH):
        for side in range(2):
            field_halo[q][side].wait_recv()
            widen(frecv.at[side], xpad, q * rows, rows, 2 * lon_dev * side)
        for h in range(halves):
            wide = [wlon[h, k] for k in range(KW)]

            @pl.loop(q * rows, (q + 1) * rows)
            def _(i):
                v = lon_taps(xpad, wide, i, h, False).astype(BF)
                abf[i, :, h * 128:(h + 1) * 128] = v
                aband[h, HALF + i] = v.astype(F32)

    def lat_start(src, dst, ss, rs):
        @pl.when(my + 1 < n_lat)
        def _():
            remote(src.at[pl.ds(lat_dev - HALF, HALF)], dst.at[0], ss.at[0], rs.at[0], me, my + 1).start()

        @pl.when(my > 0)
        def _():
            remote(src.at[pl.ds(0, HALF)], dst.at[1], ss.at[1], rs.at[1], me, my - 1).start()

    def lat_finish(src, dst, wide, ss, rs):
        for side, has in ((0, my > 0), (1, my + 1 < n_lat)):
            base = side * (HALF + lat_dev)

            @pl.when(has)
            def _():
                remote(src.at[pl.ds(0, HALF)], dst.at[side], ss.at[side], rs.at[side], me, lax.rem(my + 1, n_lat)).wait_recv()

                @pl.loop(0, HALF)
                def _(i):
                    v = dst[side, i].astype(F32)
                    for h in range(halves):
                        wide[h, base + i] = v[:, h * 128:(h + 1) * 128]

            @pl.when(jnp.logical_not(has))
            def _():
                @pl.loop(0, HALF)
                def _(i):
                    for h in range(halves):
                        wide[h, base + i] = jnp.zeros((lon_dev, 128), F32)

    def lat_sent(src, dst, ss, rs):
        @pl.when(my + 1 < n_lat)
        def _():
            remote(src.at[pl.ds(lat_dev - HALF, HALF)], dst.at[0], ss.at[0], rs.at[0], me, my + 1).wait_send()

        @pl.when(my > 0)
        def _():
            remote(src.at[pl.ds(0, HALF)], dst.at[1], ss.at[1], rs.at[1], me, my - 1).wait_send()

    GROUP = 4

    def lat_taps(wide_ref, ws, h, row0, flip):
        acc = [jnp.zeros((lon_dev, 128), F32)] * GROUP
        for j in range(KW - 1 + GROUP):
            x = wide_ref[h, row0 + j]
            for r in range(GROUP):
                k = j - r
                if 0 <= k < KW:
                    acc[r] = acc[r] + x * ws[KW - 1 - k if flip else k]
        return acc

    def lat_weights(h):
        return [jnp.concatenate([wlat[h, k]] * 2, axis=0) for k in range(KW)]

    lat_start(abf, arecv, a_ss, a_rs)
    lat_finish(abf, arecv, aband, a_ss, a_rs)
    for h in range(halves):
        ws = lat_weights(h)

        @pl.loop(0, lat_dev // GROUP)
        def _(g):
            acc = lat_taps(aband, ws, h, g * GROUP, False)
            for r in range(GROUP):
                mixed[g * GROUP + r, :, h * 128:(h + 1) * 128] = acc[r]

    tile = 16
    cells = tile * lon_dev

    @pl.loop(0, lat_dev // tile)
    def _(t):
        lats = pl.ds(t * tile, tile)
        rws = pl.ds(pl.multiple_of(t * cells, cells), cells)
        mix = mixed[lats].reshape(cells, chans)
        inv = 1.0 / jnp.sqrt(jnp.mean(mix * mix, axis=-1, keepdims=True) + 1e-6)
        unit = mix * inv
        nrm = unit.astype(BF)
        normed[rws, :] = nrm
        ct = cot[lats].reshape(cells, chans)
        res = field[lats].reshape(cells, chans).astype(F32)
        dn = jnp.zeros((cells, chans), F32)
        for b in range(hidden // 256):
            blk = slice(b * 256, (b + 1) * 256)
            x = jnp.dot(nrm, w_in[:, blk], preferred_element_type=F32)
            da = jnp.dot(ct, w_out_t[:, blk], preferred_element_type=F32)
            xx = x * x
            th = jnp.tanh(x * (ROOT + (ROOT * 0.044715) * xx))
            hp = 0.5 + 0.5 * th
            a = (x * hp).astype(BF)
            slope = hp + (0.5 * x) * (1.0 - th * th) * (ROOT + (3.0 * ROOT * 0.044715) * xx)
            dp = (da * slope).astype(BF)
            act[rws, blk] = a
            dpre[rws, blk] = dp
            res = res + jnp.dot(a, w_out[blk, :], preferred_element_type=F32)
            dn = dn + jnp.dot(dp, w_in_t[blk, :], preferred_element_type=F32)
        result[lats] = res.astype(BF).reshape(tile, lon_dev, chans)
        dm = ((dn - unit * jnp.mean(dn * unit, axis=-1, keepdims=True)) * inv).astype(BF)
        dm = dm.reshape(tile, lon_dev, chans)
        abf_m = dm.astype(F32)
        for h in range(halves):
            dband[h, pl.ds(HALF + t * tile, tile)] = abf_m[:, :, h * 128:(h + 1) * 128]
        dmbf[lats] = dm

    lat_start(dmbf, mrecv, m_ss, m_rs)

    for b in range(hidden // 256):
        blk = slice(b * 256, (b + 1) * 256)
        part_b[blk, :] = lax.dot_general(
            act[:, blk], cot[...].reshape(lat_dev * lon_dev, chans),
            (((0,), (0,)), ((), ())), preferred_element_type=F32).astype(BF)
        part_b[hidden + b * 256:hidden + (b + 1) * 256, :] = lax.dot_general(
            normed[...], dpre[:, blk],
            (((0,), (0,)), ((), ())), preferred_element_type=F32).astype(BF)

    def reduction(part, lrecv, pair, nrecv, whole, sub, lss, lrs, nss, nrs, ass, ars, gss, grs):
        per_lat = part.shape[0] // n_lat
        owners = per_lat // sub
        mine = pl.multiple_of(my * per_lat, 16)
        has = me < owners

        def lat_copy(p):
            to = lax.rem(my + p, n_lat)
            src = part.at[pl.ds(pl.multiple_of(to * per_lat, 16), per_lat)]
            return remote(src, lrecv.at[p - 1], lss.at[p - 1], lrs.at[p - 1], me, to)

        def lon_copy(p):
            to = lax.rem(me + p, n_lon)
            src = pair.at[pl.ds(pl.multiple_of(lax.rem(to, owners) * sub, 16), sub)]
            return to, remote(src, nrecv.at[p - 1], nss.at[p - 1], nrs.at[p - 1], to, my)

        def own_rows(lon):
            return pl.ds(pl.multiple_of(mine + lax.rem(lon, owners) * sub, 16), sub)

        def gather_copy(p, lon):
            ref = whole.at[own_rows(lon)]
            return remote(ref, ref, ass.at[p - 1], ars.at[p - 1], lax.rem(me + p, n_lon), my)

        def spread_copy(p, lat):
            ref = whole.at[pl.ds(pl.multiple_of(lat * per_lat, 16), per_lat)]
            return remote(ref, ref, gss.at[p - 1], grs.at[p - 1], me, lax.rem(my + p, n_lat))

        def step1():
            @pl.loop(1, n_lat)
            def _(p):
                lat_copy(p).start()

        def step2():
            @pl.loop(1, n_lat)
            def _(p):
                lat_copy(p).wait_recv()
            total = part[pl.ds(mine, per_lat), :].astype(F32)
            for p in range(1, n_lat):
                total = total + lrecv[p - 1].astype(F32)
            pair[...] = total.astype(BF)

            @pl.loop(1, n_lon)
            def _(p):
                to, c = lon_copy(p)

                @pl.when(to < owners)
                def _():
                    c.start()

        def step3():
            @pl.when(has)
            def _():
                @pl.loop(1, n_lon)
                def _(p):
                    lon_copy(p)[1].wait_recv()
                rows_own = pl.ds(pl.multiple_of(lax.rem(me, owners) * sub, 16), sub)
                total = pair[rows_own, :].astype(F32)
                total = lax.fori_loop(
                    0, n_lon - 1, lambda p, v: v + nrecv[p].astype(F32), total)
                whole[own_rows(me), :] = total.astype(BF)

                @pl.loop(1, n_lon)
                def _(p):
                    gather_copy(p, me).start()

        def step4():
            @pl.loop(1, n_lon)
            def _(p):
                source = lax.rem(me + n_lon - p, n_lon)

                @pl.when(source < owners)
                def _():
                    gather_copy(p, source).wait_recv()

            @pl.loop(1, n_lat)
            def _(p):
                spread_copy(p, my).start()

        def step5():
            @pl.loop(1, n_lat)
            def _(p):
                spread_copy(p, lax.rem(my + n_lat - p, n_lat)).wait_recv()

        def done():
            @pl.loop(1, n_lat)
            def _(p):
                lat_copy(p).wait_send()
                spread_copy(p, my).wait_send()

            @pl.loop(1, n_lon)
            def _(p):
                to, c = lon_copy(p)

                @pl.when(to < owners)
                def _():
                    c.wait_send()

                @pl.when(has)
                def _():
                    gather_copy(p, me).wait_send()

        return step1, step2, step3, step4, step5, done

    big = reduction(part_b, lrecv_b, pair_b, nrecv_b, all_b, subs[0],
                    b_lss, b_lrs, b_nss, b_nrs, b_ass, b_ars, b_gss, b_grs)
    small = reduction(part_s, lrecv_s, pair_s, nrecv_s, all_s, subs[1],
                      s_lss, s_lrs, s_nss, s_nrs, s_ass, s_ars, s_gss, s_grs)
    big[0]()

    lat_finish(dmbf, mrecv, dband, m_ss, m_rs)
    d_halo = [lon_halo(dalbf, drecv, d_ss, d_rs, q) for q in range(CH)]
    for q in range(CH):
        for h in range(halves):
            ws = lat_weights(h)

            @pl.loop(0, rows // GROUP)
            def _(g):
                row0 = q * rows + g * GROUP
                acc = lat_taps(dband, ws, h, row0, True)
                for r in range(GROUP):
                    v = acc[r].astype(BF)
                    dalbf[row0 + r, :, h * 128:(h + 1) * 128] = v
                    ypad[h, row0 + r, lon_dev:2 * lon_dev, :] = v.astype(F32)
        for c in d_halo[q]:
            c.start()
    big[1]()

    part_s[...] = jnp.zeros(part_s.shape, BF)

    def tap_grads(load_d, load_x, base):
        for h in range(halves):
            def body(i, accs):
                d = load_d(h, i)
                d0, d1 = d[:8], d[8:]
                out = []
                for k in range(KW):
                    x0, x1 = load_x(h, i, k)
                    out.append(accs[k] + (x0 * d0 + x1 * d1))
                return tuple(out)

            accs = lax.fori_loop(0, lat_dev, body, (jnp.zeros((8, 128), F32),) * KW)
            sums = [jnp.sum(a, axis=0, keepdims=True) for a in accs]
            sums.append(jnp.zeros((1, 128), F32))
            part_s[base:base + 32, h * 128:(h + 1) * 128] = jnp.concatenate(sums, axis=0).astype(BF)

    def lat_x(h, i, k):
        v = aband[h, i + k]
        return v[:8], v[8:]

    tap_grads(lambda h, i: dband[h, HALF + i], lat_x, 0)
    tap_grads(
        lambda h, i: ypad[h, i, lon_dev:2 * lon_dev, :],
        lambda h, i, k: (xpad[h, i, k + 1:k + 9, :], xpad[h, i, k + 9:k + 17, :]),
        32,
    )
    small[0]()
    big[2]()
    small[1]()

    for q in range(CH):
        for side in range(2):
            d_halo[q][side].wait_recv()
            widen(drecv.at[side], ypad, q * rows, rows, 2 * lon_dev * side)
        if q == 1:
            small[2]()
        if q == 2:
            big[3]()
        for h in range(halves):
            wide = [wlon[h, k] for k in range(KW)]
            lanes = slice(h * 128, (h + 1) * 128)

            @pl.loop(q * rows, (q + 1) * rows)
            def _(i):
                v = lon_taps(ypad, wide, i, h, True)
                d_field[i, :, lanes] = (cot[i, :, lanes].astype(F32) + v).astype(BF)

    small[3]()
    big[4]()
    out_big[...] = all_b[...]
    small[4]()
    out_small[...] = all_s[...]
    big[5]()
    small[5]()
    for pair in field_halo + d_halo:
        for c in pair:
            c.wait_send()
    lat_sent(abf, arecv, a_ss, a_rs)
    lat_sent(dmbf, mrecv, m_ss, m_rs)


def split_rows(total, n_lon, n_lat):
    per_lat = total // n_lat
    sub = max(16, per_lat // n_lon)
    assert per_lat % sub == 0 and sub % 16 == 0 and per_lat // sub <= n_lon
    return per_lat, sub


def on_device(n_lon, n_lat, field, cotangent, lon_kernel, lat_kernel, w_in, w_out):
    lat_dev, lon_dev, chans = field.shape
    hidden = w_in.shape[1]
    halves = chans // 128
    cells = lat_dev * lon_dev
    scale = 1.0 / math.sqrt(cells * n_lon * n_lat)
    big = 2 * hidden
    small = max(64, 16 * n_lat)
    big_lat, big_sub = split_rows(big, n_lon, n_lat)
    small_lat, small_sub = split_rows(small, n_lon, n_lat)
    sem = pltpu.SemaphoreType.DMA

    def buffers(total, per_lat, sub):
        return [
            pltpu.VMEM((total, chans), BF),
            pltpu.VMEM((max(n_lat - 1, 1), per_lat, chans), BF),
            pltpu.VMEM((per_lat, chans), BF),
            pltpu.VMEM((n_lon - 1, sub, chans), BF),
            pltpu.VMEM((total, chans), BF),
        ]

    sems = [sem((n_lat,))] * 2 + [sem((n_lon,))] * 4 + [sem((n_lat,))] * 2
    block = (lat_dev, lon_dev, chans)
    result, d_field, all_big, all_small = pl.pallas_call(
        functools.partial(kernel, n_lon, n_lat, (big_sub, small_sub)),
        out_shape=[
            jax.ShapeDtypeStruct(block, BF),
            jax.ShapeDtypeStruct(block, BF),
            jax.ShapeDtypeStruct((big, chans), BF),
            jax.ShapeDtypeStruct((small, chans), BF),
        ],
        in_specs=[pl.BlockSpec(memory_space=pltpu.VMEM)] * 6,
        out_specs=[pl.BlockSpec(memory_space=pltpu.VMEM)] * 4,
        scratch_shapes=[
            pltpu.VMEM((halves, lat_dev, 3 * lon_dev, 128), F32),
            pltpu.VMEM((halves, lat_dev, 3 * lon_dev, 128), F32),
            pltpu.VMEM((halves, lat_dev + 2 * HALF, lon_dev, 128), F32),
            pltpu.VMEM((halves, lat_dev + 2 * HALF, lon_dev, 128), F32),
            pltpu.VMEM(block, F32),
            pltpu.VMEM(block, BF),
            pltpu.VMEM(block, BF),
            pltpu.VMEM((2,) + block, BF),
            pltpu.VMEM((2,) + block, BF),
            pltpu.VMEM((2, HALF, lon_dev, chans), BF),
            pltpu.VMEM((2, HALF, lon_dev, chans), BF),
            pltpu.VMEM((halves, KW, 8, 128), F32),
            pltpu.VMEM((halves, KW, 8, 128), F32),
            pltpu.VMEM((hidden, chans), BF),
            pltpu.VMEM((chans, hidden), BF),
            pltpu.VMEM((cells, hidden), BF),
            pltpu.VMEM((cells, hidden), BF),
            pltpu.VMEM((cells, chans), BF),
            pltpu.VMEM(block, BF),
        ]
        + buffers(big, big_lat, big_sub)
        + buffers(small, small_lat, small_sub)
        + [sem((2, CH))] * 4
        + [sem((2,))] * 4
        + sems
        + sems,
        compiler_params=pltpu.CompilerParams(
            collective_id=0, has_side_effects=True, vmem_limit_bytes=56 * 1024 * 1024
        ),
    )(field, cotangent, lon_kernel, lat_kernel, w_in, w_out)
    grad_out = scale * all_big[:hidden].astype(F32)
    grad_in = scale * (
        all_big[hidden:].reshape(hidden // 256, chans, 256).transpose(1, 0, 2)
        .reshape(chans, hidden).astype(F32)
    )
    grad_lat = scale * all_small[:KW].astype(F32)
    grad_lon = scale * all_small[32:32 + KW].astype(F32)
    return (result, d_field, grad_in, grad_out, grad_lat, grad_lon)


def solution(mesh):
    placed = (P("lat", "lon", None), P("lat", "lon", None), P(), P(), P(), P())
    return jax.shard_map(
        functools.partial(on_device, mesh.shape["lon"], mesh.shape["lat"]),
        mesh=mesh,
        in_specs=placed,
        out_specs=(P("lat", "lon", None), P("lat", "lon", None), P(), P(), P(), P()),
        check_vma=False,
    )
```

time: 252 us -> 106 us (0.42)
  Pallas kernels: 0 us -> 98.5 us
  other arithmetic: 70 us -> 2.99 us
  waiting for transfers between devices: 61.3 us -> 0 us
  blocking collectives: 52.1 us -> 0 us
  starting transfers between devices: 21.1 us -> 0 us
  local copies, waits for them, and re-layouts: 18 us -> 3.14 us
  between operations: 15.4 us -> 0.65 us
  matrix products: 13.5 us -> 0 us
    pallas_call x0 -> x1, Pallas kernels: none -> 98.5 us  [on_device(): pl.pallas_call(functools.partial(kernel, n_lon, n_lat, (big_sub, small_su...]
    reduce_sum x8 -> x0, other arithmetic: 56.1 us -> none  [the longest x7 34.7 us: kernel_grad(): rows_out.append(jnp.sum(piece * grad_wide, axis=(0, 1)))]
    psum x1 -> x0, blocking collectives: 52.1 us -> none  [on_device(): lax.psum((grad_in, grad_out, grad_lat, grad_lon), ('lon', 'lat'))]
    psum x1 -> x0, waiting for transfers between devices: 45.3 us -> none  [on_device(): lax.psum((grad_in, grad_out, grad_lat, grad_lon), ('lon', 'lat'))]
    ppermute x8 -> x0, starting transfers between devices: 21 us -> none  [the longest x4 10.9 us: with_halo(): after = lax.ppermute(initial, axis, down)]
    ppermute x8 -> x0, waiting for transfers between devices: 15.9 us -> none  [the longest x4 15.9 us: with_halo(): after = lax.ppermute(initial, axis, down)]
    dot_general x6 -> x0, matrix products: 13.5 us -> none  [the longest x1 3.4 us: mlp_block(): lax.dot_general(cot_rows, w_out, (((1,), (1,)), ((), ())), preferred_elem...]
    convert_element_type x2 -> x0, other arithmetic: 12.3 us -> none  [the longest x1 6.96 us: on_device(): d_field = (cotangent.astype(jnp.float32) + conv_back).astype(jnp.bfloat16)]
  transfers between devices with their start and end apart: 9 -> 0, of which waited for: 3 -> 0; matrix products, arithmetic and copies ran while one was open for 17% -> 0% of each run, Pallas kernels for 0% -> 0%
where the time goes in v1:
time: 106 us; the launch traced here: 105 us
  Pallas kernels  98.5 us (93%)
  local copies, waits for them, and re-layouts  3.14 us (3%)
  other arithmetic  2.99 us (3%)
    pallas_call x1, Pallas kernels, on_device(): pl.pallas_call(functools.partial(kernel, n_lon, n_lat, (big_sub, small_su...  98.5 us
    mul x1, other arithmetic, on_device(): grad_out = scale * all_big[:hidden].astype(F32)  2.36 us

profile of v1, /device:TPU:0, one launch (start us, length us, event | category | flops | bytes accessed | tf_op | source)
XLA Modules:
  0.0 105.3 jit_solution(18241617958905874902)
XLA Ops:
  0.6 98.5 %shard_map.109 = (bf16[64,16,256]{2,1,0:T(8,128)(2,1)}, bf16[64,16,256]{2,1,0:T(8,128)(2,1)}, bf16[2048,256]{1,0:T(8,128)(2,1)}, bf16[64,256]{1,0:T(8,128)(2,1)}) custom-call(bf16[64,16,256]{2,1,0:T(8,128)(2,1)} %field.1, bf16[64,16,256]{2,1,0:T(8,128)(2,1)} %cot.1, f32[31,256]{1,0:T(8,128)} %lon_k.1, f32[31,256]{1,0:T(8,128)} %lat_k.1, ...), custom_call_target="tpu_custom_call" | custom-call | tf_op jit(solution)/shard_map/pallas_call | solution.py:446
  99.2 2.4 %convert_multiply_fusion = (f32[1024,256]{1,0:T(8,128)}, f32[1024,256]{1,0:T(8,128)S(1)}) fusion(bf16[2048,256]{1,0:T(8,128)(2,1)} %get-tuple-element.12), kind=kLoop, calls=%fused_computation | loop fusion | flops 1048576 | bytes 3145728 | tf_op jit(solution)/shard_map/mul | solution.py:487
  101.5 0.0 copy-start.2
  101.5 0.0 copy-start.1
  101.5 1.1 %copy.13 = f32[4,32,8,256]{3,2,0,1:T(8,128)} copy(f32[4,32,8,256]{3,2,1,0:T(8,128)S(1)} %bitcast.5) | data formatting | bytes 2097152 | tf_op jit(solution)/shard_map/mul | solution.py:488
  102.6 0.0 copy-done.2
  102.6 0.6 convert_multiply_fusion.2
  103.3 0.0 copy-done.1
  103.3 0.0 copy-start
  103.3 0.8 copy.16
  104.1 0.4 copy-done
  104.5 0.8 copy.17
Async XLA Ops:
  101.5 1.1 %copy-start.2 = (bf16[64,256]{1,0:T(8,128)(2,1)S(1)}, bf16[64,256]{1,0:T(8,128)(2,1)}, u32[]{:S(2)}) copy-start(bf16[64,256]{1,0:T(8,128)(2,1)} %get-tuple-element.13) | copy-start | bytes 98308
  101.5 1.7 %copy-start.1 = (bf16[64,16,256]{2,1,0:T(8,128)(2,1)S(1)}, bf16[64,16,256]{2,1,0:T(8,128)(2,1)}, u32[]{:S(2)}) copy-start(bf16[64,16,256]{2,1,0:T(8,128)(2,1)} %get-tuple-element.24) | copy-start | bytes 1572868
  103.3 1.2 %copy-start = (bf16[64,16,256]{2,1,0:T(8,128)(2,1)S(1)}, bf16[64,16,256]{2,1,0:T(8,128)(2,1)}, u32[]{:S(2)}) copy-start(bf16[64,16,256]{2,1,0:T(8,128)(2,1)} %get-tuple-element.25) | copy-start | bytes 1572868

commit v2 on v1

--- a/solution.py
+++ b/solution.py
@@ -71,9 +71,13 @@
             for h in range(halves):
                 pad[h, row0 + i, col:col + lon_dev, :] = v[:, h * 128:(h + 1) * 128]
 
-    field_halo = [lon_halo(field, frecv, f_ss, f_rs, q) for q in range(CH)]
-    for pair in field_halo:
-        for c in pair:
+    even = lax.rem(my, 2) == 0
+
+    def order(q):
+        return jnp.where(even, CH - 1 - q, q)
+
+    for q in range(CH):
+        for c in lon_halo(field, frecv, f_ss, f_rs, order(q)):
             c.start()
 
     for h in range(halves):
@@ -96,34 +100,21 @@
             hi = hi + pad[h, i, off + 8:off + 16, :] * wide[k]
         return jnp.concatenate([lo, hi], axis=0)
 
-    band = [[0, HALF], [HALF + lat_dev, HALF]]
-    for q in range(CH):
-        for side in range(2):
-            field_halo[q][side].wait_recv()
-            widen(frecv.at[side], xpad, q * rows, rows, 2 * lon_dev * side)
-        for h in range(halves):
-            wide = [wlon[h, k] for k in range(KW)]
-
-            @pl.loop(q * rows, (q + 1) * rows)
-            def _(i):
-                v = lon_taps(xpad, wide, i, h, False).astype(BF)
-                abf[i, :, h * 128:(h + 1) * 128] = v
-                aband[h, HALF + i] = v.astype(F32)
-
-    def lat_start(src, dst, ss, rs):
-        @pl.when(my + 1 < n_lat)
+    def edge_start(q, src, dst, ss, rs):
+        @pl.when(jnp.logical_and(q == CH - 1, my + 1 < n_lat))
         def _():
             remote(src.at[pl.ds(lat_dev - HALF, HALF)], dst.at[0], ss.at[0], rs.at[0], me, my + 1).start()
 
-        @pl.when(my > 0)
+        @pl.when(jnp.logical_and(q == 0, my > 0))
         def _():
             remote(src.at[pl.ds(0, HALF)], dst.at[1], ss.at[1], rs.at[1], me, my - 1).start()
 
-    def lat_finish(src, dst, wide, ss, rs):
+    def edge_finish(q, src, dst, wide, ss, rs):
         for side, has in ((0, my > 0), (1, my + 1 < n_lat)):
             base = side * (HALF + lat_dev)
-
-            @pl.when(has)
+            here = q == side * (CH - 1)
+
+            @pl.when(jnp.logical_and(here, has))
             def _():
                 remote(src.at[pl.ds(0, HALF)], dst.at[side], ss.at[side], rs.at[side], me, lax.rem(my + 1, n_lat)).wait_recv()
 
@@ -133,12 +124,28 @@
                     for h in range(halves):
                         wide[h, base + i] = v[:, h * 128:(h + 1) * 128]
 
-            @pl.when(jnp.logical_not(has))
+            @pl.when(jnp.logical_and(here, jnp.logical_not(has)))
             def _():
                 @pl.loop(0, HALF)
                 def _(i):
                     for h in range(halves):
                         wide[h, base + i] = jnp.zeros((lon_dev, 128), F32)
+
+    def lon_forward(q):
+        for c in lon_halo(field, frecv, f_ss, f_rs, q):
+            c.wait_recv()
+        for side in range(2):
+            widen(frecv.at[side], xpad, q * rows, rows, 2 * lon_dev * side)
+        for h in range(halves):
+            wide = [wlon[h, k] for k in range(KW)]
+
+            @pl.loop(0, rows)
+            def _(r):
+                i = q * rows + r
+                v = lon_taps(xpad, wide, i, h, False).astype(BF)
+                abf[i, :, h * 128:(h + 1) * 128] = v
+                aband[h, HALF + i] = v.astype(F32)
+        edge_start(q, abf, arecv, a_ss, a_rs)
 
     def lat_sent(src, dst, ss, rs):
         @pl.when(my + 1 < n_lat)
@@ -164,22 +171,21 @@
     def lat_weights(h):
         return [jnp.concatenate([wlat[h, k]] * 2, axis=0) for k in range(KW)]
 
-    lat_start(abf, arecv, a_ss, a_rs)
-    lat_finish(abf, arecv, aband, a_ss, a_rs)
-    for h in range(halves):
-        ws = lat_weights(h)
-
-        @pl.loop(0, lat_dev // GROUP)
-        def _(g):
-            acc = lat_taps(aband, ws, h, g * GROUP, False)
-            for r in range(GROUP):
-                mixed[g * GROUP + r, :, h * 128:(h + 1) * 128] = acc[r]
-
-    tile = 16
+    tile = rows
     cells = tile * lon_dev
 
-    @pl.loop(0, lat_dev // tile)
-    def _(t):
+    def mlp(t):
+        edge_finish(t, abf, arecv, aband, a_ss, a_rs)
+        for h in range(halves):
+            ws = lat_weights(h)
+
+            @pl.loop(0, tile // GROUP)
+            def _(g):
+                row0 = t * tile + g * GROUP
+                acc = lat_taps(aband, ws, h, row0, False)
+                for r in range(GROUP):
+                    mixed[row0 + r, :, h * 128:(h + 1) * 128] = acc[r]
+
         lats = pl.ds(t * tile, tile)
         rws = pl.ds(pl.multiple_of(t * cells, cells), cells)
         mix = mixed[lats].reshape(cells, chans)
@@ -211,8 +217,37 @@
         for h in range(halves):
             dband[h, pl.ds(HALF + t * tile, tile)] = abf_m[:, :, h * 128:(h + 1) * 128]
         dmbf[lats] = dm
-
-    lat_start(dmbf, mrecv, m_ss, m_rs)
+        edge_start(t, dmbf, mrecv, m_ss, m_rs)
+
+    def lat_backward(q):
+        edge_finish(q, dmbf, mrecv, dband, m_ss, m_rs)
+        for h in range(halves):
+            ws = lat_weights(h)
+
+            @pl.loop(0, rows // GROUP)
+            def _(g):
+                row0 = q * rows + g * GROUP
+                acc = lat_taps(dband, ws, h, row0, True)
+                for r in range(GROUP):
+                    v = acc[r].astype(BF)
+                    dalbf[row0 + r, :, h * 128:(h + 1) * 128] = v
+                    ypad[h, row0 + r, lon_dev:2 * lon_dev, :] = v.astype(F32)
+        for c in lon_halo(dalbf, drecv, d_ss, d_rs, q):
+            c.start()
+
+    @pl.loop(0, CH + 1)
+    def _(s):
+        @pl.when(s < CH)
+        def _():
+            lon_forward(order(s))
+
+        @pl.when(s >= 1)
+        def _():
+            mlp(order(s - 1))
+
+        @pl.when(s >= 2)
+        def _():
+            lat_backward(order(s - 2))
 
     for b in range(hidden // 256):
         blk = slice(b * 256, (b + 1) * 256)
@@ -332,23 +367,8 @@
                       s_lss, s_lrs, s_nss, s_nrs, s_ass, s_ars, s_gss, s_grs)
     big[0]()
 
-    lat_finish(dmbf, mrecv, dband, m_ss, m_rs)
-    d_halo = [lon_halo(dalbf, drecv, d_ss, d_rs, q) for q in range(CH)]
-    for q in range(CH):
-        for h in range(halves):
-            ws = lat_weights(h)
-
-            @pl.loop(0, rows // GROUP)
-            def _(g):
-                row0 = q * rows + g * GROUP
-                acc = lat_taps(dband, ws, h, row0, True)
-                for r in range(GROUP):
-                    v = acc[r].astype(BF)
-                    dalbf[row0 + r, :, h * 128:(h + 1) * 128] = v
-                    ypad[h, row0 + r, lon_dev:2 * lon_dev, :] = v.astype(F32)
-        for c in d_halo[q]:
-            c.start()
     big[1]()
+    lat_backward(order(CH - 1))
 
     part_s[...] = jnp.zeros(part_s.shape, BF)
 
@@ -379,35 +399,39 @@
         32,
     )
     small[0]()
-    big[2]()
-    small[1]()
-
-    for q in range(CH):
+
+    def lon_backward(q):
+        for c in lon_halo(dalbf, drecv, d_ss, d_rs, q):
+            c.wait_recv()
         for side in range(2):
-            d_halo[q][side].wait_recv()
             widen(drecv.at[side], ypad, q * rows, rows, 2 * lon_dev * side)
-        if q == 1:
-            small[2]()
-        if q == 2:
-            big[3]()
         for h in range(halves):
             wide = [wlon[h, k] for k in range(KW)]
             lanes = slice(h * 128, (h + 1) * 128)
 
-            @pl.loop(q * rows, (q + 1) * rows)
-            def _(i):
+            @pl.loop(0, rows)
+            def _(r):
+                i = q * rows + r
                 v = lon_taps(ypad, wide, i, h, True)
                 d_field[i, :, lanes] = (cot[i, :, lanes].astype(F32) + v).astype(BF)
 
+    big[2]()
+    small[1]()
+    lon_backward(order(0))
+    lon_backward(order(1))
+    small[2]()
+    lon_backward(order(2))
+    big[3]()
     small[3]()
+    lon_backward(order(3))
+    small[4]()
+    out_small[...] = all_s[...]
     big[4]()
     out_big[...] = all_b[...]
-    small[4]()
-    out_small[...] = all_s[...]
     big[5]()
     small[5]()
-    for pair in field_halo + d_halo:
-        for c in pair:
+    for q in range(CH):
+        for c in lon_halo(field, frecv, f_ss, f_rs, q) + lon_halo(dalbf, drecv, d_ss, d_rs, q):
             c.wait_send()
     lat_sent(abf, arecv, a_ss, a_rs)
     lat_sent(dmbf, mrecv, m_ss, m_rs)

time: 106 us -> 87.5 us (0.83)
  Pallas kernels: 98.5 us -> 80.5 us
    pallas_call x1, Pallas kernels: 98.5 us -> 80.5 us  [on_device(): pl.pallas_call(functools.partial(kernel, n_lon, n_lat, (big_sub, small_su...]
where the time goes in v2:
time: 87.5 us; the launch traced here: 87.3 us
  Pallas kernels  80.5 us (92%)
  local copies, waits for them, and re-layouts  3.14 us (4%)
  other arithmetic  2.99 us (3%)
    pallas_call x1, Pallas kernels, on_device(): pl.pallas_call(functools.partial(kernel, n_lon, n_lat, (big_sub, small_su...  80.5 us
    mul x1, other arithmetic, on_device(): grad_out = scale * all_big[:hidden].astype(F32)  2.36 us
    unnamed x8, local copies, waits for them, and re-layouts  2.03 us

profile of v2, /device:TPU:0, one launch (start us, length us, event | category | flops | bytes accessed | tf_op | source)
XLA Modules:
  0.0 87.3 jit_solution(2695653121723868185)
XLA Ops:
  0.6 80.5 %shard_map.109 = (bf16[64,16,256]{2,1,0:T(8,128)(2,1)}, bf16[64,16,256]{2,1,0:T(8,128)(2,1)}, bf16[2048,256]{1,0:T(8,128)(2,1)}, bf16[64,256]{1,0:T(8,128)(2,1)}) custom-call(bf16[64,16,256]{2,1,0:T(8,128)(2,1)} %field.1, bf16[64,16,256]{2,1,0:T(8,128)(2,1)} %cot.1, f32[31,256]{1,0:T(8,128)} %lon_k.1, f32[31,256]{1,0:T(8,128)} %lat_k.1, ...), custom_call_target="tpu_custom_call" | custom-call | tf_op jit(solution)/shard_map/pallas_call | solution.py:470
  81.2 2.4 %convert_multiply_fusion = (f32[1024,256]{1,0:T(8,128)}, f32[1024,256]{1,0:T(8,128)S(1)}) fusion(bf16[2048,256]{1,0:T(8,128)(2,1)} %get-tuple-element.12), kind=kLoop, calls=%fused_computation | loop fusion | flops 1048576 | bytes 3145728 | tf_op jit(solution)/shard_map/mul | solution.py:511
  83.5 0.0 copy-start.2
  83.5 0.0 copy-start.1
  83.5 1.1 %copy.13 = f32[4,32,8,256]{3,2,0,1:T(8,128)} copy(f32[4,32,8,256]{3,2,1,0:T(8,128)S(1)} %bitcast.5) | data formatting | bytes 2097152 | tf_op jit(solution)/shard_map/mul | solution.py:512
  84.6 0.0 copy-done.2
  84.6 0.6 convert_multiply_fusion.2
  85.3 0.0 copy-done.1
  85.3 0.0 copy-start
  85.3 0.8 copy.16
  86.1 0.4 copy-done
  86.5 0.8 copy.17
Async XLA Ops:
  83.5 1.1 %copy-start.2 = (bf16[64,256]{1,0:T(8,128)(2,1)S(1)}, bf16[64,256]{1,0:T(8,128)(2,1)}, u32[]{:S(2)}) copy-start(bf16[64,256]{1,0:T(8,128)(2,1)} %get-tuple-element.13) | copy-start | bytes 98308
  83.5 1.7 %copy-start.1 = (bf16[64,16,256]{2,1,0:T(8,128)(2,1)S(1)}, bf16[64,16,256]{2,1,0:T(8,128)(2,1)}, u32[]{:S(2)}) copy-start(bf16[64,16,256]{2,1,0:T(8,128)(2,1)} %get-tuple-element.24) | copy-start | bytes 1572868
  85.3 1.2 %copy-start = (bf16[64,16,256]{2,1,0:T(8,128)(2,1)S(1)}, bf16[64,16,256]{2,1,0:T(8,128)(2,1)}, u32[]{:S(2)}) copy-start(bf16[64,16,256]{2,1,0:T(8,128)(2,1)} %get-tuple-element.25) | copy-start | bytes 1572868
